TPU v7x, 32 devices: a whole 2x2x4 slice. The times are simulated.
32 devices in a mesh: dp: 16 (over z, y, x), tensor: 2 (over core).
Axes of the slice: x: 2, y: 2, z: 4, core: 2. Of those that a mesh axis runs over, the one named last changes fastest.
Arguments:
- inputs: bfloat16 [8192, 768], P(('dp', 'tensor')), may hold values from -6 to 6
- segments: int32 [8192], P('dp'), may hold values from 0 to 2, as said below
- gain_first: float32 [768], P(('dp', 'tensor')), may hold values from 0.5 to 1.5
- gain_second: float32 [768], P(('dp', 'tensor')), may hold values from 0.5 to 1.5
- attend_weight: bfloat16 [3, 768, 768], P(None, 'dp', 'tensor'), may hold values from -0.21875 to 0.21875
- mixing_matrix: bfloat16 [768, 768], P('dp', 'tensor'), may hold values from -0.875 to 0.875
- expand_matrix: bfloat16 [2, 768, 1152], P(None, 'dp', 'tensor'), may hold values from -0.21875 to 0.21875
- reduce_matrix: bfloat16 [768, 1152], P('dp', 'tensor'), may hold values from -0.1875 to 0.1875
- cotangent: bfloat16 [8192, 768], P(('dp', 'tensor')), may hold values from -6 to 6
Outputs:
- output: bfloat16 [8192, 768], P(('dp', 'tensor'))
- input_grad: float32 [8192, 768], P(('dp', 'tensor'))
- first_grad: float32 [768], P(('dp', 'tensor'))
- second_grad: float32 [768], P(('dp', 'tensor'))
- attend_grad: float32 [3, 768, 768], P(None, 'dp', 'tensor')
- mixing_grad: float32 [768, 768], P('dp', 'tensor')
- expand_grad: float32 [2, 768, 1152], P(None, 'dp', 'tensor')
- reduce_grad: float32 [768, 1152], P('dp', 'tensor')
Inputs may be any that keep to these rules, and one draw needn't show every extreme that they name: `segments`: in each aligned block of 512 tokens (one sequence) the numbers start at 0, never fall and rise by one at two places, so each sequence holds three documents of 128 tokens or more; the middle one covers positions 255 and 256 of its sequence.
All inputs are finite; a program needn't handle non-finite values.
Results may differ from a plain program's by a relative error of at most 0.018.
Values may be sent and summed in bfloat16 or wider, within the bound.
A program may use at most 128 MiB of HBM per device.

v0:
```python
import math

import jax
import jax.numpy as jnp
from jax import lax
from jax.sharding import PartitionSpec as P

HEAD_SIZE = 64


EPS = 1e-05
THETA = 160000.0
MASKED = -1e30


def rotary_tables(length, head_size):
    indices = jnp.arange(head_size // 2, dtype=jnp.float32)
    inverse_freq = THETA ** (-(2.0 / head_size) * indices)
    angles = jnp.arange(length, dtype=jnp.float32)[:, None] * inverse_freq[None, :]
    angles = jnp.concatenate([angles, angles], axis=1)
    return (jnp.cos(angles), jnp.sin(angles))


def rotate_half(values):
    midway = values.shape[-1] // 2
    return jnp.concatenate([-values[..., midway:], values[..., :midway]], axis=-1)


def rotate(values, cosine_table, sine_table):
    return values * cosine_table + rotate_half(values) * sine_table


def rotate_back(grad_values, cosine_table, sine_table):
    return grad_values * cosine_table - rotate_half(grad_values * sine_table)


def normalize(values):
    centered = values - jnp.mean(values, axis=-1, keepdims=True)
    inverse_std = lax.rsqrt(jnp.mean(centered * centered, axis=-1, keepdims=True) + EPS)
    return (centered * inverse_std, inverse_std)


def normalize_back(grad_unit, unit_rows, inverse_std):
    plain_mean = jnp.mean(grad_unit, axis=-1, keepdims=True)
    cross_mean = jnp.mean(grad_unit * unit_rows, axis=-1, keepdims=True)
    return inverse_std * (grad_unit - plain_mean - unit_rows * cross_mean)


def contract_last(left_side, right_side):
    return lax.dot_general(
        left_side, right_side, (((1,), (1,)), ((), ())), preferred_element_type=jnp.float32
    )


def contract_first(left_side, right_side):
    return lax.dot_general(
        left_side, right_side, (((0,), (0,)), ((), ())), preferred_element_type=jnp.float32
    )


def gelu_slope(values):
    return 0.5 * (1.0 + lax.erf(values / math.sqrt(2.0))) + values * jnp.exp(
        -0.5 * values * values
    ) / math.sqrt(2.0 * math.pi)


def per_device(
    inputs,
    segments,
    gain_first,
    gain_second,
    attend_weight,
    mixing_matrix,
    expand_matrix,
    reduce_matrix,
    cotangent,
):
    full_first, full_second = (
        lax.all_gather(gain_first, ("dp", "tensor"), axis=0, tiled=True),
        lax.all_gather(gain_second, ("dp", "tensor"), axis=0, tiled=True),
    )
    attend_full, mixing_full, expand_full, reduce_full = (
        lax.all_gather(attend_weight, "dp", axis=1, tiled=True),
        lax.all_gather(mixing_matrix, "dp", axis=0, tiled=True),
        lax.all_gather(expand_matrix, "dp", axis=1, tiled=True),
        lax.all_gather(reduce_matrix, "dp", axis=0, tiled=True),
    )
    length = segments.shape[0]
    local_width = attend_full.shape[2]
    local_heads = local_width // HEAD_SIZE
    score_scale = HEAD_SIZE ** (-0.5)
    cosine_table, sine_table = rotary_tables(length, HEAD_SIZE)
    cosine_table = cosine_table[:, None, :]
    sine_table = sine_table[:, None, :]
    same_doc = segments[:, None] == segments[None, :]

    def split_heads(flat_rows):
        return flat_rows.reshape(length, local_heads, HEAD_SIZE)

    def swap_heads(split_rows):
        return jnp.transpose(split_rows, (1, 0, 2))

    def attend_head(per_head):
        query_head, key_head, value_head = per_head
        masked = jnp.where(same_doc, contract_last(query_head, key_head), MASKED)
        row_peak = jnp.max(masked, axis=-1, keepdims=True)
        exponent = jnp.exp(masked - row_peak)
        denominator = jnp.sum(exponent, axis=-1, keepdims=True)
        softmax_low = (exponent / denominator).astype(jnp.bfloat16)
        mixed_head = jnp.dot(softmax_low, value_head, preferred_element_type=jnp.float32)
        return (mixed_head.astype(jnp.bfloat16), (row_peak + jnp.log(denominator))[:, 0])

    def attend_back(per_head):
        query_head, key_head, value_head, grad_head, log_total = per_head
        masked = jnp.where(same_doc, contract_last(query_head, key_head), MASKED)
        softmax_out = jnp.exp(masked - log_total[:, None])
        grad_value = contract_first(softmax_out.astype(jnp.bfloat16), grad_head).astype(
            jnp.bfloat16
        )
        grad_softmax = contract_last(grad_head, value_head)
        inner_sum = jnp.sum(grad_softmax * softmax_out, axis=-1, keepdims=True)
        grad_scores = (softmax_out * (grad_softmax - inner_sum)).astype(jnp.bfloat16)
        grad_query = jnp.dot(grad_scores, key_head, preferred_element_type=jnp.float32)
        grad_key = contract_first(grad_scores, query_head)
        return (grad_query, grad_key, grad_value)

    rows_in = inputs.astype(jnp.float32)
    unit_one, inverse_one = normalize(rows_in)
    first_normed = (unit_one * full_first).astype(jnp.bfloat16)
    gathered_one = lax.all_gather(first_normed, "tensor", axis=0, tiled=True)
    query_raw = split_heads(
        jnp.dot(gathered_one, attend_full[0], preferred_element_type=jnp.float32)
    )
    key_raw = split_heads(jnp.dot(gathered_one, attend_full[1], preferred_element_type=jnp.float32))
    value_raw = jnp.dot(gathered_one, attend_full[2], preferred_element_type=jnp.float32).astype(
        jnp.bfloat16
    )
    query_heads = swap_heads(
        (rotate(query_raw, cosine_table, sine_table) * score_scale).astype(jnp.bfloat16)
    )
    key_heads = swap_heads(rotate(key_raw, cosine_table, sine_table).astype(jnp.bfloat16))
    value_heads = swap_heads(split_heads(value_raw))
    mixed_heads, log_totals = lax.map(attend_head, (query_heads, key_heads, value_heads))
    attended_rows = swap_heads(mixed_heads).reshape(length, local_width)
    picked = attended_rows
    middle = rows_in + lax.psum_scatter(
        contract_last(picked, mixing_full).astype(jnp.bfloat16),
        "tensor",
        scatter_dimension=0,
        tiled=True,
    ).astype(jnp.float32)
    unit_two, inverse_two = normalize(middle)
    second_normed = (unit_two * full_second).astype(jnp.bfloat16)
    gathered_two = lax.all_gather(second_normed, "tensor", axis=0, tiled=True)
    activated_input = jnp.dot(gathered_two, expand_full[0], preferred_element_type=jnp.float32)
    gate_projected = jnp.dot(gathered_two, expand_full[1], preferred_element_type=jnp.float32)
    gelu_value = jax.nn.gelu(activated_input, approximate=False)
    hidden_rows = (gelu_value * gate_projected).astype(jnp.bfloat16)
    picked = hidden_rows
    output = middle + lax.psum_scatter(
        contract_last(picked, reduce_full).astype(jnp.bfloat16),
        "tensor",
        scatter_dimension=0,
        tiled=True,
    ).astype(jnp.float32)
    back_attend, back_mixing, back_expand, back_reduce = (
        lax.all_gather(attend_weight, "dp", axis=1, tiled=True),
        lax.all_gather(mixing_matrix, "dp", axis=0, tiled=True),
        lax.all_gather(expand_matrix, "dp", axis=1, tiled=True),
        lax.all_gather(reduce_matrix, "dp", axis=0, tiled=True),
    )
    grad_out_rows = lax.all_gather(cotangent, "tensor", axis=0, tiled=True)
    grad_hidden = jnp.dot(grad_out_rows, back_reduce, preferred_element_type=jnp.float32)
    grad_reduce = contract_first(grad_out_rows, hidden_rows)
    grad_activated = (grad_hidden * gate_projected * gelu_slope(activated_input)).astype(
        jnp.bfloat16
    )
    grad_gate = (grad_hidden * gelu_value).astype(jnp.bfloat16)
    grad_expand = jnp.stack(
        [contract_first(gathered_two, grad_activated), contract_first(gathered_two, grad_gate)]
    )
    grad_normed_two = lax.psum_scatter(
        (
            contract_last(grad_activated, back_expand[0]) + contract_last(grad_gate, back_expand[1])
        ).astype(jnp.bfloat16),
        "tensor",
        scatter_dimension=0,
        tiled=True,
    ).astype(jnp.float32)
    second_local = jnp.sum(grad_normed_two * unit_two, axis=0)
    grad_middle = cotangent.astype(jnp.float32) + normalize_back(
        grad_normed_two * full_second, unit_two, inverse_two
    )
    grad_branch = grad_middle.astype(jnp.bfloat16)
    grad_mid_rows = lax.all_gather(grad_branch, "tensor", axis=0, tiled=True)
    grad_attended = jnp.dot(grad_mid_rows, back_mixing, preferred_element_type=jnp.float32).astype(
        jnp.bfloat16
    )
    grad_mixing = contract_first(grad_mid_rows, attended_rows)
    grad_heads = swap_heads(split_heads(grad_attended))
    grad_query, grad_key, grad_value = lax.map(
        attend_back, (query_heads, key_heads, value_heads, grad_heads, log_totals)
    )
    grad_query_raw = rotate_back(swap_heads(grad_query) * score_scale, cosine_table, sine_table)
    grad_query_raw = grad_query_raw.reshape(length, local_width).astype(jnp.bfloat16)
    grad_key_raw = rotate_back(swap_heads(grad_key), cosine_table, sine_table)
    grad_key_raw = grad_key_raw.reshape(length, local_width).astype(jnp.bfloat16)
    grad_value_raw = swap_heads(grad_value).reshape(length, local_width)
    grad_attend = jnp.stack(
        [
            contract_first(gathered_one, grad_query_raw),
            contract_first(gathered_one, grad_key_raw),
            contract_first(gathered_one, grad_value_raw),
        ]
    )
    grad_normed_one = lax.psum_scatter(
        (
            contract_last(grad_query_raw, back_attend[0])
            + contract_last(grad_key_raw, back_attend[1])
            + contract_last(grad_value_raw, back_attend[2])
        ).astype(jnp.bfloat16),
        "tensor",
        scatter_dimension=0,
        tiled=True,
    ).astype(jnp.float32)
    first_local = jnp.sum(grad_normed_one * unit_one, axis=0)
    input_grad = grad_middle + normalize_back(grad_normed_one * full_first, unit_one, inverse_one)
    sent_attend, sent_mixing, sent_expand, sent_reduce = (
        lax.psum_scatter(grad_attend, "dp", scatter_dimension=1, tiled=True),
        lax.psum_scatter(grad_mixing, "dp", scatter_dimension=0, tiled=True),
        lax.psum_scatter(grad_expand, "dp", scatter_dimension=1, tiled=True),
        lax.psum_scatter(grad_reduce, "dp", scatter_dimension=0, tiled=True),
    )
    first_grad, second_grad = (
        lax.psum_scatter(first_local, ("dp", "tensor"), scatter_dimension=0, tiled=True),
        lax.psum_scatter(second_local, ("dp", "tensor"), scatter_dimension=0, tiled=True),
    )
    return (
        output.astype(jnp.bfloat16),
        input_grad,
        first_grad,
        second_grad,
        sent_attend,
        sent_mixing,
        sent_expand,
        sent_reduce,
    )


def solution(mesh):
    in_specs = (
        P(("dp", "tensor"), None),
        P("dp"),
        P(("dp", "tensor")),
        P(("dp", "tensor")),
        P(None, "dp", "tensor"),
        P("dp", "tensor"),
        P(None, "dp", "tensor"),
        P("dp", "tensor"),
        P(("dp", "tensor"), None),
    )
    out_specs = (
        P(("dp", "tensor"), None),
        P(("dp", "tensor"), None),
        P(("dp", "tensor")),
        P(("dp", "tensor")),
        P(None, "dp", "tensor"),
        P("dp", "tensor"),
        P(None, "dp", "tensor"),
        P("dp", "tensor"),
    )
    return jax.shard_map(
        per_device, mesh=mesh, in_specs=in_specs, out_specs=out_specs, check_vma=False
    )
```

profile of v0, /device:TPU:0, one launch (start us, length us, event | category | flops | bytes accessed | tf_op | source)
XLA Modules:
  0.0 888.3 jit_solution(13553994678261108076)
XLA Ops:
  9.7 42.8 %all-reduce.6 = (f32[768]{0:T(1024)S(1)}, f32[768]{0:T(1024)S(1)}) all-reduce(f32[768]{0:T(1024)S(1)} %dynamic-update-slice.1, f32[768]{0:T(1024)S(1)} %dynamic-update-slice), channel_id=1, replica_groups=mesh['dp'=16,'tensor'=2] {'dp','tensor'}, use_global_device_ids=true, to_apply=%add.1 | all-reduce | flops 1536 | bytes 12288
  55.2 2.4 all_gather.35
  57.6 45.2 %all_gather.37 = bf16[768,384]{1,0:T(8,128)(2,1)} all-gather(bf16[48,384]{1,0:T(8,128)(2,1)S(1)} %copy-done.42), channel_id=1, replica_groups=mesh['dp'=16,'tensor'=2] {'dp'}, dimensions={0}, use_global_device_ids=true | all-gather | bytes 626688 | tf_op jit(solution)/shard_map/all_gather | solution.py:84
  113.3 24.0 %while.28 = (s32[]{:T(128)}, bf16[6,512,64]{1,2,0:T(8,128)(2,1)S(1)}, f32[6,512]{1,0:T(8,128)}, bf16[6,512,64]{2,1,0:T(8,128)(2,1)}, bf16[6,512,64]{2,1,0:T(8,12...) while((s32[]{:T(128)}, ...), condition=%wide.region_5.6_spmd.clone, body=%wide.region_2.5_spmd.clone.sunk | while | flops 69238272 | bytes 3631209 | solution.py:143
  137.3 2.7 convolution_convert_fusion.3
  140.9 2.5 all_gather.42
  143.4 44.7 %all_gather.41 = bf16[768,576]{1,0:T(8,128)(2,1)} all-gather(bf16[48,576]{1,0:T(8,128)(2,1)S(1)} %copy-done.41), channel_id=1, replica_groups=mesh['dp'=16,'tensor'=2] {'dp'}, dimensions={0}, use_global_device_ids=true | all-gather | bytes 940032 | tf_op jit(solution)/shard_map/all_gather | solution.py:86
  190.8 2.5 all_gather.39
  193.4 17.3 %all-gather.5.cloned.1.call-done = bf16[2,768,576]{2,1,0:T(8,128)(2,1)} async-done(((bf16[2,48,576]{2,1,0:T(8,128)(2,1)}), bf16[2,768,576]{2,1,0:T(8,128)(2,1)}) %all-gather.5.cloned.1.call-update) | async-done | bytes 1769488 | tf_op jit(solution)/shard_map/all_gather | solution.py:85
  210.7 2.0 fusion.69
  214.6 4.6 multiply_convert_fusion.1
  222.0 7.0 reduce-scatter.14.cloned.1.call-done
  229.0 2.1 fusion.79
  233.4 2.4 all_gather.43
  238.4 44.9 %while.29 = (s32[]{:T(128)}, f32[6,512,64]{1,2,0:T(8,128)}, f32[6,512,64]{1,2,0:T(8,128)}, bf16[6,512,64]{1,2,0:T(8,128)(2,1)S(1)}, bf16[6,512,64]{2,1,0:T(8,128...) while((s32[]{:T(128)}, f32[6,512,64]{1,2,0:T(8,128)}, ...), condition=%wide.region_15.16_spmd.clone, body=%wide.region_13.15_spmd.clone.sunk | while | flops 170163712 | bytes 9129081 | solution.py:201
  243.1 1.9 fusion.172
  250.6 1.9 fusion.172
  258.1 1.8 fusion.172
  265.6 1.9 fusion.172
  273.0 1.8 fusion.172
  280.5 1.9 fusion.172
  297.6 2.0 pad_maximum_fusion.1
  299.6 7.5 copy.35
  308.4 1.9 convolution_bitcast_fusion.4
  310.3 2.9 copy.38
  319.3 2.1 pad_maximum_fusion
  324.8 44.6 %all-reduce.5 = (f32[768]{0:T(1024)S(1)}, f32[768]{0:T(1024)S(1)}) all-reduce(f32[768]{0:T(1024)S(1)} %get-tuple-element.197, f32[768]{0:T(1024)S(1)} %copy-done.49), channel_id=6, replica_groups=mesh['dp'=16,'tensor'=2] {'dp','tensor'}, use_global_device_ids=true, to_apply=%region_20.21.clone | all-reduce | flops 1536 | bytes 12288
  370.6 2.8 fusion.73
  373.3 110.3 %all-reduce.9.cloned.1.call-done = f32[2,768,576]{2,0,1:T(2,128)} async-done(((f32[2,768,576]{2,0,1:T(2,128)}), f32[2,768,576]{2,0,1:T(2,128)}) %all-reduce.9.cloned.1.call-update) | async-done | bytes 3538960
  485.3 128.9 %reduce-scatter.22.cloned.1.call-done = f32[48,576]{1,0:T(8,128)} async-done(((f32[768,576]{1,0:T(8,128)}), f32[48,576]{1,0:T(8,128)}) %reduce-scatter.22.cloned.1.call-update) | async-done | bytes 110608
  614.2 128.5 %reduce-scatter.20.cloned.1.call-done = f32[48,384]{1,0:T(8,128)} async-done(((f32[768,384]{1,0:T(8,128)}), f32[48,384]{1,0:T(8,128)}) %reduce-scatter.20.cloned.1.call-update) | async-done | bytes 73744 | tf_op jit(solution)/shard_map/reduce_scatter | solution.py:230
  742.7 138.8 %reduce-scatter.18.cloned.1.call-done = f32[3,48,384]{2,1,0:T(8,128)} async-done(((f32[3,768,384]{2,1,0:T(8,128)}), f32[3,48,384]{2,1,0:T(8,128)}) %reduce-scatter.18.cloned.1.call-update) | async-done | bytes 221200 | tf_op jit(solution)/shard_map/reduce_scatter | solution.py:229
  (266 shorter events, 113.1 us)
Async XLA Ops:
  7.2 47.5 %copy-start = (bf16[256,768]{1,0:T(8,128)(2,1)S(1)}, bf16[256,768]{1,0:T(8,128)(2,1)}, u32[]{:S(2)}) copy-start(bf16[256,768]{1,0:T(8,128)(2,1)} %param.13) | copy-start | bytes 1179652
  7.2 95.6 %all-gather.3.cloned.1.call-start = ((), (), s32[]{:S(2)}) async-start(), calls=%async_computation.7 | async-start | bytes 1880064 | tf_op jit(solution)/shard_map/all_gather | solution.py:83
  7.9 180.2 %reduce-scatter.10.cloned.1.call-start = ((), (), s32[]{:S(2)}) async-start(), calls=%async_computation.8 | async-start | bytes 1179648 | tf_op jit(solution)/shard_map/reduce_scatter | solution.py:146
  54.7 2.9 copy-start.43
  54.7 2.9 copy-start.42
  55.0 47.8 %copy-start.47 = (f32[256]{0:T(256)}, f32[256]{0:T(256)S(1)}, u32[]{:S(2)}) copy-start(f32[256]{0:T(256)S(1)} %add_rsqrt_fusion.1) | copy-start | bytes 3076
  110.7 2.6 copy-start.40
  137.3 2.8 copy-start.13
  137.3 3.5 copy-start.15
  140.0 3.4 copy-start.41
  140.1 70.6 %all-gather.5.cloned.1.call-start = ((), (), s32[]{:S(2)}) async-start(), calls=%async_computation.9 | async-start | bytes 2088960 | tf_op jit(solution)/shard_map/all_gather | solution.py:85
  140.8 88.2 %reduce-scatter.14.cloned.1.call-start = ((), (), s32[]{:S(2)}) async-start(), calls=%async_computation.11 | async-start | bytes 1179648 | tf_op jit(solution)/shard_map/reduce_scatter | solution.py:182
  188.1 2.5 copy-start.1
  190.6 2.8 copy-start.45
  210.7 2.0 copy-start.2
  221.9 10.4 %copy-start.16 = (bf16[256,768]{1,0:T(8,128)(2,1)S(1)}, bf16[256,768]{1,0:T(8,128)(2,1)}, u32[]{:S(2)}) copy-start(bf16[256,768]{1,0:T(8,128)(2,1)} %param.21) | copy-start | bytes 1179652
  221.9 101.4 %reduce-scatter.16.cloned.1.call-start = ((), (), s32[]{:S(2)}) async-start(), calls=%async_computation.12 | async-start | bytes 1179648 | tf_op jit(solution)/shard_map/reduce_scatter | solution.py:216
  229.0 3.3 copy-start.18
  232.3 4.4 copy-start.26
  291.7 78.8 %reduce-scatter.12.cloned.1.call-start = ((), (), s32[]{:S(2)}) async-start(), calls=%async_computation.10 | async-start | bytes 1179648 | tf_op jit(solution)/shard_map/reduce_scatter | solution.py:160
  291.8 2.4 copy-start.38
  294.2 2.0 copy-start.30
  295.9 187.7 %all-reduce.9.cloned.1.call-start = ((), (), s32[]{:S(2)}) async-start(), calls=%async_computation.16 | async-start | bytes 7864320
  307.1 307.1 %reduce-scatter.22.cloned.1.call-start = ((), (), s32[]{:S(2)}) async-start(), calls=%async_computation.15 | async-start | bytes 2088960
  313.2 429.5 %reduce-scatter.20.cloned.1.call-start = ((), (), s32[]{:S(2)}) async-start(), calls=%async_computation.14 | async-start | bytes 1253376 | tf_op jit(solution)/shard_map/reduce_scatter | solution.py:230
  316.1 565.4 %reduce-scatter.18.cloned.1.call-start = ((), (), s32[]{:S(2)}) async-start(), calls=%async_computation.13 | async-start | bytes 3760128 | tf_op jit(solution)/shard_map/reduce_scatter | solution.py:229
  321.4 3.4 copy-start.49
  321.4 49.2 %copy-start.17 = (bf16[256,768]{1,0:T(8,128)(2,1)S(1)}, bf16[256,768]{1,0:T(8,128)(2,1)}, u32[]{:S(2)}) copy-start(bf16[256,768]{1,0:T(8,128)(2,1)} %param.21) | copy-start | bytes 1179652
  321.4 49.2 %copy-start.19 = (bf16[256,768]{1,0:T(8,128)(2,1)S(1)}, bf16[256,768]{1,0:T(8,128)(2,1)}, u32[]{:S(2)}) copy-start(bf16[256,768]{1,0:T(8,128)(2,1)} %reduce-scatter.14.cloned.1.call-done) | copy-start | bytes 1179652
  321.4 49.2 %copy-start.46 = (f32[256]{0:T(256)S(1)}, f32[256]{0:T(256)}, u32[]{:S(2)}) copy-start(f32[256]{0:T(256)} %copy-done.45) | copy-start | bytes 3076
  321.4 49.2 %copy-start.51 = (f32[256]{0:T(256)S(1)}, f32[256]{0:T(256)}, u32[]{:S(2)}) copy-start(f32[256]{0:T(256)} %copy-done.50) | copy-start | bytes 3076
  321.4 49.2 %copy-start.53 = (f32[256]{0:T(256)S(1)}, f32[256]{0:T(256)}, u32[]{:S(2)}) copy-start(f32[256]{0:T(256)} %copy-done.52) | copy-start | bytes 3076
  (33 other events, 39.3 us)
Sparse Core Ops, SparseCore 0:
  10.7 63.7 all-gather.2
  140.2 4.1 reduce-scatter.9
  147.4 63.2 all-gather.4
  222.0 6.9 reduce-scatter.13
  291.8 9.3 reduce-scatter.15
  303.4 9.3 reduce-scatter.11
  318.7 164.9 all-reduce.8
  489.1 125.0 reduce-scatter.21
  620.2 122.4 reduce-scatter.19
  749.0 132.4 reduce-scatter.17
where the time goes:
time: 891 us; the launch traced here: 888 us
  waiting for transfers between devices  532 us (60%)
  blocking collectives  187 us (21%)
  matrix products  80.1 us (9%)
  local copies, waits for them, and re-layouts  47.9 us (5%)
  other arithmetic  24.6 us (3%)
  between operations  15.5 us (2%)
    unnamed x12, waiting for transfers between devices  241 us
    reduce_scatter x1, waiting for transfers between devices, per_device(): lax.psum_scatter(grad_attend, 'dp', scatter_dimension=1, tiled=True)  139 us
    reduce_scatter x1, waiting for transfers between devices, per_device(): lax.psum_scatter(grad_mixing, 'dp', scatter_dimension=0, tiled=True)  129 us
    unnamed x2, blocking collectives  87.4 us
    all_gather x1, blocking collectives, per_device(): lax.all_gather(mixing_matrix, 'dp', axis=0, tiled=True)  45.2 us
    all_gather x1, blocking collectives, per_device(): lax.all_gather(reduce_matrix, 'dp', axis=0, tiled=True)  44.7 us
    dot_general x25, matrix products, contract_last(): lax.dot_general(left_side, right_side, (((1,), (1,)), ((), ())), preferre...  32.2 us
    dot_general x19, matrix products, contract_first(): lax.dot_general(left_side, right_side, (((0,), (0,)), ((), ())), preferre...  24.9 us
  transfers between devices with their start and end apart: 10, of which 6 were waited for; matrix products, arithmetic and copies ran while one was open for 4% of the time, Pallas kernels for 0%

commit v1 on v0

v1 whole, which is shorter than its diff:
```python
import functools
import math

import jax
import jax.numpy as jnp
from jax import lax
from jax.experimental import pallas as pl
from jax.experimental.pallas import tpu as pltpu
from jax.sharding import PartitionSpec as P

HEAD_SIZE = 64
EPS = 1e-05
THETA = 160000.0
MASKED = -1e30
LANES = 128
VMEM_LIMIT = 60 * 1024 * 1024
MESH = pl.DeviceIdType.MESH
VMEM = pltpu.VMEM


def normalize(values):
    centered = values - jnp.mean(values, axis=-1, keepdims=True)
    inverse_std = lax.rsqrt(jnp.mean(centered * centered, axis=-1, keepdims=True) + EPS)
    return (centered * inverse_std, inverse_std)


def normalize_back(grad_unit, unit_rows, inverse_std):
    plain_mean = jnp.mean(grad_unit, axis=-1, keepdims=True)
    cross_mean = jnp.mean(grad_unit * unit_rows, axis=-1, keepdims=True)
    return inverse_std * (grad_unit - plain_mean - unit_rows * cross_mean)


def plain(left_side, right_side):
    return jnp.dot(left_side, right_side, preferred_element_type=jnp.float32)


def contract_last(left_side, right_side):
    return lax.dot_general(
        left_side, right_side, (((1,), (1,)), ((), ())), preferred_element_type=jnp.float32
    )


def contract_first(left_side, right_side):
    return lax.dot_general(
        left_side, right_side, (((0,), (0,)), ((), ())), preferred_element_type=jnp.float32
    )


def gelu_slope(values):
    return 0.5 * (1.0 + lax.erf(values / math.sqrt(2.0))) + values * jnp.exp(
        -0.5 * values * values
    ) / math.sqrt(2.0 * math.pi)


def position():
    dp, core = lax.axis_index("dp"), lax.axis_index("tensor")
    zh, zl = lax.rem(lax.div(dp, 8), 2), lax.rem(lax.div(dp, 4), 2)
    y, x = lax.rem(lax.div(dp, 2), 2), lax.rem(dp, 2)
    peers = dict(
        core=(dp, 1 - core),
        x=(dp + 1 - 2 * x, core),
        y=(dp + 2 - 4 * y, core),
        zl=(dp + 4 - 8 * zl, core),
        zh=(dp + 8 - 16 * zh, core),
    )
    return core, zh, zl, y, x, peers


def greet(peers):
    barrier = pltpu.get_barrier_semaphore()
    for peer in peers.values():
        pl.semaphore_signal(barrier, inc=1, device_id=peer, device_id_type=MESH)
    pl.semaphore_wait(barrier, len(peers))


def gather_kernel(chunks, *refs):
    kinds = 1 + max(kind for kind, _ in chunks)
    shards, tokens = refs[:kinds], refs[kinds]
    fulls, other_tokens = refs[kinds + 1 : 2 * kinds + 1], refs[2 * kinds + 1]
    own_sem, send_sem, recv_sem, token_sem = refs[2 * kinds + 2 :]
    core, zh, zl, y, x, peers = position()
    every = slice(None)

    def remote(k, slot, source, target, peer):
        return pltpu.make_async_remote_copy(
            src_ref=source,
            dst_ref=target,
            send_sem=send_sem.at[k, slot],
            recv_sem=recv_sem.at[k, slot],
            device_id=peers[peer],
            device_id_type=MESH,
        )

    def same(k, slot, index, peer):
        kind, j = chunks[k]
        block = fulls[kind].at[(core, j) + index]
        return remote(k, slot, block, block, peer)

    own = []
    for k, (kind, j) in enumerate(chunks):
        own.append(
            pltpu.make_async_copy(
                shards[kind].at[j], fulls[kind].at[core, j, zh, zl, y, x], own_sem.at[k]
            )
        )
    stages = [[] for _ in chunks]
    for k, (kind, j) in enumerate(chunks):
        stages[k] = [
            [
                remote(
                    k, 0, shards[kind].at[j], fulls[kind].at[core, j, zh, zl, y, x], "zh"
                )
            ],
            [same(k, 1, (every, zl, y, x), "zl")],
            [same(k, 2, (every, 0, y, x), "x"), same(k, 3, (every, 1, y, x), "y")],
            [same(k, 4, (every, 0, y), "y"), same(k, 5, (every, 1, every, x), "x")],
            [same(k, 6, (), "core")],
        ]
    token_copy = pltpu.make_async_remote_copy(
        src_ref=tokens,
        dst_ref=other_tokens,
        send_sem=token_sem.at[0],
        recv_sem=token_sem.at[1],
        device_id=peers["core"],
        device_id_type=MESH,
    )
    for copy in own:
        copy.start()
    greet(peers)
    token_copy.start()
    count, depth = len(chunks), 5
    for step in range(count + depth):
        for stage in range(depth, -1, -1):
            k = step - stage
            if 0 <= k < count:
                if stage > 0:
                    for copy in stages[k][stage - 1]:
                        copy.wait_recv()
                if stage == 1:
                    own[k].wait()
                if stage < depth:
                    for copy in stages[k][stage]:
                        copy.start()
    for per_chunk in stages:
        for group in per_chunk:
            for copy in group:
                copy.wait_send()
    token_copy.wait()


def gather_all(shards, chunks, tokens):
    blocks = [
        jax.ShapeDtypeStruct((2, s.shape[0], 2, 2, 2, 2) + s.shape[1:], s.dtype) for s in shards
    ]
    anywhere = pl.BlockSpec(memory_space=pl.ANY)
    count = len(chunks)
    out = pl.pallas_call(
        functools.partial(gather_kernel, chunks),
        out_shape=blocks + [jax.ShapeDtypeStruct(tokens.shape, tokens.dtype)],
        in_specs=[anywhere] * (len(shards) + 1),
        out_specs=[anywhere] * (len(shards) + 1),
        scratch_shapes=[
            pltpu.SemaphoreType.DMA((count,)),
            pltpu.SemaphoreType.DMA((count, 7)),
            pltpu.SemaphoreType.DMA((count, 7)),
            pltpu.SemaphoreType.DMA((2,)),
        ],
        compiler_params=pltpu.CompilerParams(
            collective_id=0, has_side_effects=True, vmem_limit_bytes=VMEM_LIMIT
        ),
    )(*shards, tokens)
    fulls = [
        full.reshape((2, s.shape[0], 16 * s.shape[1], s.shape[2]))
        for full, s in zip(out[:-1], shards)
    ]
    return fulls, out[-1]


def reduce_kernel(chunks, kinds, *refs):
    parts, rows = refs[:kinds], refs[kinds]
    outs, other_rows = refs[kinds + 1 : 2 * kinds + 1], refs[2 * kinds + 1]
    refs = refs[2 * kinds + 2 :]
    sums, firsts, seconds, thirds, fourths = (
        refs[i * kinds : (i + 1) * kinds] for i in range(5)
    )
    send_sem, recv_sem, row_sem = refs[5 * kinds :]
    core, zh, zl, y, x, peers = position()
    every = slice(None)

    def remote(k, slot, source, target, peer):
        return pltpu.make_async_remote_copy(
            src_ref=source,
            dst_ref=target,
            send_sem=send_sem.at[k, slot],
            recv_sem=recv_sem.at[k, slot],
            device_id=peers[peer],
            device_id_type=MESH,
        )

    stages = []
    for k, (kind, j) in enumerate(chunks):
        part, total = parts[kind], sums[kind].at[j]
        stages.append(
            [
                [remote(k, 0, part.at[1 - core, j], total, "core")],
                [
                    remote(k, 1, total.at[every, 0, every, 1 - x], firsts[kind].at[j, 0], "x"),
                    remote(k, 2, total.at[every, 1, 1 - y], firsts[kind].at[j, 1], "y"),
                ],
                [
                    remote(k, 3, total.at[every, 0, 1 - y, x], seconds[kind].at[j, 0], "y"),
                    remote(k, 4, total.at[every, 1, y, 1 - x], seconds[kind].at[j, 1], "x"),
                ],
                [remote(k, 5, total.at[every, 1 - zl, y, x], thirds[kind].at[j], "zl")],
                [remote(k, 6, total.at[1 - zh, zl, y, x], fourths[kind].at[j], "zh")],
            ]
        )

    def add(k, stage):
        kind, j = chunks[k]
        part, total = parts[kind], sums[kind]
        if stage == 0:

            @pl.loop(0, 16)
            def _(b):
                at = (lax.div(b, 8), lax.rem(lax.div(b, 4), 2), lax.rem(lax.div(b, 2), 2), lax.rem(b, 2))
                total[(j,) + at] = total[(j,) + at] + part[(core, j) + at]

        elif stage == 1:

            @pl.loop(0, 4)
            def _(b):
                hi, lo = lax.div(b, 2), lax.rem(b, 2)
                total[j, hi, 0, lo, x] = total[j, hi, 0, lo, x] + firsts[kind][j, 0, hi, lo]
                total[j, hi, 1, y, lo] = total[j, hi, 1, y, lo] + firsts[kind][j, 1, hi, lo]

        elif stage == 2:

            @pl.loop(0, 2)
            def _(hi):
                total[j, hi, 0, y, x] = total[j, hi, 0, y, x] + seconds[kind][j, 0, hi]
                total[j, hi, 1, y, x] = total[j, hi, 1, y, x] + seconds[kind][j, 1, hi]

        elif stage == 3:

            @pl.loop(0, 2)
            def _(hi):
                total[j, hi, zl, y, x] = total[j, hi, zl, y, x] + thirds[kind][j, hi]

        else:
            outs[kind][j] = total[j, zh, zl, y, x].astype(jnp.float32) + fourths[kind][
                j
            ].astype(jnp.float32)

    row_copy = pltpu.make_async_remote_copy(
        src_ref=rows,
        dst_ref=other_rows,
        send_sem=row_sem.at[0],
        recv_sem=row_sem.at[1],
        device_id=peers["core"],
        device_id_type=MESH,
    )
    greet(peers)
    count, depth = len(chunks), 5
    for step in range(count + depth):
        for stage in range(depth, -1, -1):
            k = step - stage
            if 0 <= k < count:
                if stage > 0:
                    for copy in stages[k][stage - 1]:
                        copy.wait_recv()
                    add(k, stage - 1)
                if stage < depth:
                    for copy in stages[k][stage]:
                        copy.start()
        if step == count - 1:
            row_copy.start()
    for per_chunk in stages:
        for group in per_chunk:
            for copy in group:
                copy.wait_send()
    row_copy.wait()


def reduce_all(parts, chunks, rows):
    parts = [
        part.reshape(part.shape[:2] + (2, 2, 2, 2, part.shape[2] // 16, part.shape[3]))
        for part in parts
    ]
    kinds, count = len(parts), len(chunks)
    whole = pl.BlockSpec(memory_space=VMEM)

    def buffers(dims):
        return [VMEM((p.shape[1],) + dims + p.shape[-2:], p.dtype) for p in parts]

    out = pl.pallas_call(
        functools.partial(reduce_kernel, chunks, kinds),
        out_shape=[
            jax.ShapeDtypeStruct((p.shape[1],) + p.shape[-2:], jnp.float32) for p in parts
        ]
        + [jax.ShapeDtypeStruct(rows.shape, rows.dtype)],
        in_specs=[whole] * (kinds + 1),
        out_specs=[whole] * (kinds + 1),
        scratch_shapes=buffers((2, 2, 2, 2))
        + buffers((2, 2, 2))
        + buffers((2, 2))
        + buffers((2,))
        + buffers(())
        + [
            pltpu.SemaphoreType.DMA((count, 7)),
            pltpu.SemaphoreType.DMA((count, 7)),
            pltpu.SemaphoreType.DMA((2,)),
        ],
        compiler_params=pltpu.CompilerParams(
            collective_id=1, has_side_effects=True, vmem_limit_bytes=VMEM_LIMIT
        ),
    )(*parts, rows)
    return out[:-1], out[-1]


def half_turn(values):
    lane = lax.broadcasted_iota(jnp.int32, values.shape, 1)
    low = lax.rem(lane, HEAD_SIZE) < HEAD_SIZE // 2
    shift = HEAD_SIZE // 2
    return jnp.where(
        low, -pltpu.roll(values, LANES - shift, 1), pltpu.roll(values, shift, 1)
    )


def attend_kernel(
    normed, wq, wk, wv, cosine, sine, seg_rows, seg_cols, q_out, k_out, v_out, att_out, log_out
):
    own = q_out.shape[0]
    cos, sin = cosine[...], sine[...]
    query = plain(normed[:own], wq[0, 0])
    query = query * cos[:own] + half_turn(query) * sin[:own]
    query = (query * HEAD_SIZE**-0.5).astype(jnp.bfloat16)
    keys = plain(normed[...], wk[0, 0])
    keys = (keys * cos + half_turn(keys) * sin).astype(jnp.bfloat16)
    value = plain(normed[...], wv[0, 0]).astype(jnp.bfloat16)
    q_out[...], k_out[...], v_out[...] = query, keys, value
    allowed = seg_rows[...] == seg_cols[...]
    mixed, logs = [], []
    for head in range(LANES // HEAD_SIZE):
        part = slice(head * HEAD_SIZE, (head + 1) * HEAD_SIZE)
        scores = jnp.where(allowed, contract_last(query[:, part], keys[:, part]), MASKED)
        peak = jnp.max(scores, axis=-1, keepdims=True)
        exponent = jnp.exp(scores - peak)
        total = jnp.sum(exponent, axis=-1, keepdims=True)
        probs = (exponent / total).astype(jnp.bfloat16)
        mixed.append(plain(probs, value[:, part]).astype(jnp.bfloat16))
        logs.append(jnp.broadcast_to(peak + jnp.log(total), (own, HEAD_SIZE)))
    att_out[...] = jnp.concatenate(mixed, axis=1)
    log_out[...] = jnp.concatenate(logs, axis=1)


def attend_back_kernel(
    normed, branch, wq, wk, wv, mix, cosine, sine, seg_rows, seg_cols, q_in, k_in, v_in, att_in,
    log_in, weight_out, mix_out, normed_out,
):
    own = q_in.shape[0]
    step = pl.program_id(0)
    cos, sin = cosine[...], sine[...]
    query, keys, value = q_in[...], k_in[...], v_in[...]
    grad = plain(branch[...], mix[0, 0]).astype(jnp.bfloat16)
    allowed = seg_rows[...] == seg_cols[...]
    grad_q, grad_k, grad_v = [], [], []
    for head in range(LANES // HEAD_SIZE):
        part = slice(head * HEAD_SIZE, (head + 1) * HEAD_SIZE)
        qh, kh, vh, gh = query[:, part], keys[:, part], value[:, part], grad[:, part]
        log_total = log_in[:, head * HEAD_SIZE : head * HEAD_SIZE + 1]
        scores = jnp.where(allowed, contract_last(qh, kh), MASKED)
        probs = jnp.exp(scores - log_total)
        grad_v.append(contract_first(probs.astype(jnp.bfloat16), gh))
        grad_probs = contract_last(gh, vh)
        inner = jnp.sum(grad_probs * probs, axis=-1, keepdims=True)
        grad_scores = (probs * (grad_probs - inner)).astype(jnp.bfloat16)
        grad_q.append(plain(grad_scores, kh))
        grad_k.append(contract_first(grad_scores, qh))
    gq = jnp.concatenate(grad_q, axis=1) * HEAD_SIZE**-0.5
    gk = jnp.concatenate(grad_k, axis=1)
    gv = jnp.concatenate(grad_v, axis=1).astype(jnp.bfloat16)
    gq = (gq * cos[:own] - half_turn(gq * sin[:own])).astype(jnp.bfloat16)
    gk = (gk * cos - half_turn(gk * sin)).astype(jnp.bfloat16)
    weight_out[0, 0] = contract_first(normed[:own], gq).astype(jnp.bfloat16)
    weight_out[0, 1] = contract_first(normed[...], gk).astype(jnp.bfloat16)
    weight_out[0, 2] = contract_first(normed[...], gv).astype(jnp.bfloat16)
    mix_out[0, 0] = contract_first(branch[...], att_in[...]).astype(jnp.bfloat16)
    update = contract_last(gk, wk[0, 0]) + contract_last(gv, wv[0, 0])
    first = contract_last(gq, wq[0, 0])

    @pl.when(step == 0)
    def _():
        normed_out[...] = update

    @pl.when(step > 0)
    def _():
        normed_out[...] += update

    normed_out[:own] += first


def attention_specs(width, own, length, groups):
    def weight(j):
        return pl.BlockSpec((1, 1, width, LANES), lambda p: (p // groups, j, 0, p % groups))

    def columns(rows):
        return pl.BlockSpec((rows, LANES), lambda p: (0, p))

    def whole(*shape):
        return pl.BlockSpec(shape, lambda p: (0,) * len(shape))

    return weight, columns, whole


def attend(normed, weights, cosine, sine, seg_rows, seg_cols):
    length, width = normed.shape
    own = seg_rows.shape[0]
    groups = weights.shape[3] // LANES
    weight, columns, whole = attention_specs(width, own, length, groups)
    heads = 2 * groups * LANES
    return pl.pallas_call(
        attend_kernel,
        grid=(2 * groups,),
        out_shape=[
            jax.ShapeDtypeStruct((own, heads), jnp.bfloat16),
            jax.ShapeDtypeStruct((length, heads), jnp.bfloat16),
            jax.ShapeDtypeStruct((length, heads), jnp.bfloat16),
            jax.ShapeDtypeStruct((own, heads), jnp.bfloat16),
            jax.ShapeDtypeStruct((own, heads), jnp.float32),
        ],
        in_specs=[
            whole(length, width), weight(0), weight(1), weight(2), whole(length, LANES),
            whole(length, LANES), whole(own, 1), whole(1, length),
        ],
        out_specs=[columns(own), columns(length), columns(length), columns(own), columns(own)],
        compiler_params=pltpu.CompilerParams(vmem_limit_bytes=VMEM_LIMIT),
    )(normed, weights, weights, weights, cosine, sine, seg_rows, seg_cols)


def attend_back(normed, branch, weights, mixing, cosine, sine, seg_rows, seg_cols, saved):
    length, width = normed.shape
    own = seg_rows.shape[0]
    groups = weights.shape[3] // LANES
    weight, columns, whole = attention_specs(width, own, length, groups)
    return pl.pallas_call(
        attend_back_kernel,
        grid=(2 * groups,),
        out_shape=[
            jax.ShapeDtypeStruct((2, 3, width, groups * LANES), jnp.bfloat16),
            jax.ShapeDtypeStruct((2, 1, width, groups * LANES), jnp.bfloat16),
            jax.ShapeDtypeStruct((length, width), jnp.float32),
        ],
        in_specs=[
            whole(length, width), whole(own, width), weight(0), weight(1), weight(2), weight(0),
            whole(length, LANES), whole(length, LANES), whole(own, 1), whole(1, length),
            columns(own), columns(length), columns(length), columns(own), columns(own),
        ],
        out_specs=[
            pl.BlockSpec((1, 3, width, LANES), lambda p: (p // groups, 0, 0, p % groups)),
            weight(0),
            whole(length, width),
        ],
        compiler_params=pltpu.CompilerParams(vmem_limit_bytes=VMEM_LIMIT),
    )(normed, branch, weights, weights, weights, mixing, cosine, sine, seg_rows, seg_cols, *saved)


def rotary_tables(length, core):
    indices = jnp.arange(HEAD_SIZE // 2, dtype=jnp.float32)
    inverse_freq = THETA ** (-(2.0 / HEAD_SIZE) * indices)
    angles = jnp.arange(length, dtype=jnp.float32)[:, None] * inverse_freq[None, :]
    angles = jnp.tile(angles, (1, LANES // (HEAD_SIZE // 2)))
    return own_first(jnp.cos(angles), core), own_first(jnp.sin(angles), core)


def own_first(rows, core):
    return jnp.where(core == 0, rows, jnp.roll(rows, rows.shape[0] // 2, axis=0))


def per_device(
    doubling,
    inputs,
    segments,
    gain_first,
    gain_second,
    attend_weight,
    mixing_matrix,
    expand_matrix,
    reduce_matrix,
    cotangent,
):
    core = lax.axis_index("tensor")
    own, width = inputs.shape
    length = segments.shape[0]
    share = gain_first.shape[0]
    shards = [attend_weight, mixing_matrix[None], expand_matrix, reduce_matrix[None]]
    if doubling:
        gains = jnp.zeros((1, 8, LANES), jnp.float32)
        gains = gains.at[0, 0, :share].set(gain_first).at[0, 1, :share].set(gain_second)
        order = ((4, 0), (0, 0), (0, 1), (0, 2), (1, 0), (2, 0), (2, 1), (3, 0))
        fulls, other_inputs = gather_all(shards + [gains], order, inputs)
        attend_full, mixing_full, expand_full, reduce_full, gains = fulls
        gains = gains.reshape(2, -1, 8, LANES)[:, :, :2, :share]
        full_first, full_second = jnp.transpose(gains, (2, 1, 0, 3)).reshape(2, width)
    else:
        both = ("dp", "tensor")
        full_first = lax.all_gather(gain_first, both, axis=0, tiled=True)
        full_second = lax.all_gather(gain_second, both, axis=0, tiled=True)
        attend_full, mixing_full, expand_full, reduce_full = (
            lax.all_gather(lax.all_gather(s, "dp", axis=1, tiled=True), "tensor", axis=0)
            for s in shards
        )
        pair = lax.all_gather(inputs, "tensor", axis=0)
        other_inputs = jnp.where(core == 0, pair[1], pair[0])

    cosine, sine = rotary_tables(length, core)
    segments = own_first(segments, core)
    seg_rows, seg_cols = segments[:own, None], segments[None, :]

    rows_all = jnp.concatenate([inputs, other_inputs]).astype(jnp.float32)
    rows_in = rows_all[:own]
    unit_one, inverse_one = normalize(rows_all)
    normed_one = (unit_one * full_first).astype(jnp.bfloat16)
    saved = attend(normed_one, attend_full, cosine, sine, seg_rows, seg_cols)
    attended = saved[3]
    half = attended.shape[1] // 2
    middle = (
        rows_in
        + contract_last(attended[:, :half], mixing_full[0, 0])
        + contract_last(attended[:, half:], mixing_full[1, 0])
    )
    unit_two, inverse_two = normalize(middle)
    normed_two = (unit_two * full_second).astype(jnp.bfloat16)
    output = middle
    grad_normed_two = jnp.zeros_like(middle)
    grad_expand, grad_reduce = [], []
    for side in range(2):
        activated_in = plain(normed_two, expand_full[side, 0])
        gate_linear = plain(normed_two, expand_full[side, 1])
        gelu_value = jax.nn.gelu(activated_in, approximate=False)
        hidden = (gelu_value * gate_linear).astype(jnp.bfloat16)
        output = output + contract_last(hidden, reduce_full[side, 0])
        grad_hidden = plain(cotangent, reduce_full[side, 0])
        grad_reduce.append(contract_first(cotangent, hidden).astype(jnp.bfloat16))
        grad_activated = (grad_hidden * gate_linear * gelu_slope(activated_in)).astype(
            jnp.bfloat16
        )
        grad_gate = (grad_hidden * gelu_value).astype(jnp.bfloat16)
        grad_expand.append(contract_first(normed_two, grad_activated).astype(jnp.bfloat16))
        grad_expand.append(contract_first(normed_two, grad_gate).astype(jnp.bfloat16))
        grad_normed_two = (
            grad_normed_two
            + contract_last(grad_activated, expand_full[side, 0])
            + contract_last(grad_gate, expand_full[side, 1])
        )
    hidden_width = expand_full.shape[3]
    grad_expand = jnp.stack(grad_expand).reshape(2, 2, width, hidden_width)
    grad_reduce = jnp.stack(grad_reduce).reshape(2, 1, width, hidden_width)
    second_local = jnp.sum(grad_normed_two * unit_two, axis=0)
    grad_middle = cotangent.astype(jnp.float32) + normalize_back(
        grad_normed_two * full_second, unit_two, inverse_two
    )
    grad_branch = grad_middle.astype(jnp.bfloat16)
    grad_attend, grad_mixing, grad_normed_one = attend_back(
        normed_one, grad_branch, attend_full, mixing_full, cosine, sine, seg_rows, seg_cols, saved
    )
    first_local = jnp.sum(grad_normed_one * unit_one, axis=0)
    through = normalize_back(grad_normed_one * full_first, unit_one, inverse_one)
    rows_mine = grad_middle + through[:own]
    rows_other = through[own:].astype(jnp.bfloat16)
    if doubling:
        local = jnp.stack([first_local, second_local]).reshape(2, -1, 2, share)
        local = jnp.transpose(local, (2, 1, 0, 3))
        local = jnp.pad(local, ((0, 0), (0, 0), (0, 6), (0, LANES - share)))
        local = local.reshape(2, 1, -1, LANES)
        order = ((3, 0), (2, 0), (2, 1), (0, 0), (0, 1), (0, 2), (1, 0), (4, 0))
        sent, rows_back = reduce_all(
            [grad_attend, grad_mixing, grad_expand, grad_reduce, local], order, rows_other
        )
        sent_attend, sent_mixing, sent_expand, sent_reduce, gains = sent
        sent_mixing, sent_reduce = sent_mixing[0], sent_reduce[0]
        first_grad, second_grad = gains[0, 0, :share], gains[0, 1, :share]
    else:

        def summed(part):
            part = part.astype(jnp.float32)
            part = lax.psum_scatter(part, "tensor", scatter_dimension=0, tiled=False)
            return lax.psum_scatter(part, "dp", scatter_dimension=1, tiled=True)

        sent_attend, sent_expand = summed(grad_attend), summed(grad_expand)
        sent_mixing, sent_reduce = summed(grad_mixing)[0], summed(grad_reduce)[0]
        first_grad, second_grad = (
            lax.psum_scatter(part, ("dp", "tensor"), scatter_dimension=0, tiled=True)
            for part in (first_local, second_local)
        )
        pair = lax.all_gather(rows_other, "tensor", axis=0)
        rows_back = jnp.where(core == 0, pair[1], pair[0])
    input_grad = rows_mine + rows_back.astype(jnp.float32)
    return (
        output.astype(jnp.bfloat16),
        input_grad,
        first_grad,
        second_grad,
        sent_attend,
        sent_mixing,
        sent_expand,
        sent_reduce,
    )


def solution(mesh):
    in_specs = (
        P(("dp", "tensor"), None),
        P("dp"),
        P(("dp", "tensor")),
        P(("dp", "tensor")),
        P(None, "dp", "tensor"),
        P("dp", "tensor"),
        P(None, "dp", "tensor"),
        P("dp", "tensor"),
        P(("dp", "tensor"), None),
    )
    out_specs = (
        P(("dp", "tensor"), None),
        P(("dp", "tensor"), None),
        P(("dp", "tensor")),
        P(("dp", "tensor")),
        P(None, "dp", "tensor"),
        P("dp", "tensor"),
        P(None, "dp", "tensor"),
        P("dp", "tensor"),
    )
    doubling = mesh.shape["dp"] == 16 and mesh.shape["tensor"] == 2
    return jax.shard_map(
        functools.partial(per_device, doubling),
        mesh=mesh,
        in_specs=in_specs,
        out_specs=out_specs,
        check_vma=False,
    )
```

time: 891 us -> 248 us (0.28)
  waiting for transfers between devices: 532 us -> 0 us
  Pallas kernels: 0 us -> 192 us
  blocking collectives: 187 us -> 0 us
  matrix products: 80.1 us -> 17 us
  local copies, waits for them, and re-layouts: 47.9 us -> 21.3 us
  between operations: 15.5 us -> 1.24 us
  other arithmetic: 24.6 us -> 15.6 us
    reduce_scatter x6 -> x0, waiting for transfers between devices: 274 us -> none  [the longest x1 139 us: per_device(): lax.psum_scatter(grad_attend, 'dp', scatter_dimension=1, tiled=True)]
    unnamed x12 -> x0, waiting for transfers between devices: 241 us -> none
    pallas_call x0 -> x4, Pallas kernels: none -> 192 us  [the longest x1 80.3 us: gather_all(): pl.pallas_call(functools.partial(gather_kernel, chunks), out_shape=blocks...]
    all_gather x6 -> x0, blocking collectives: 99.7 us -> none  [the longest x1 45.2 us: per_device(): lax.all_gather(mixing_matrix, 'dp', axis=0, tiled=True)]
    unnamed x2 -> x0, blocking collectives: 87.4 us -> none
    dot_general x25 -> x8, matrix products: 32.2 us -> 6.61 us  [contract_last(): lax.dot_general(left_side, right_side, (((1,), (1,)), ((), ())), preferre...]
    dot_general x19 -> x6, matrix products: 24.9 us -> 3.5 us  [contract_first(): lax.dot_general(left_side, right_side, (((0,), (0,)), ((), ())), preferre...]
    unnamed x122 -> x52, local copies, waits for them, and re-layouts: 23.7 us -> 4.71 us
  transfers between devices with their start and end apart: 10 -> 0, of which waited for: 6 -> 0; matrix products, arithmetic and copies ran while one was open for 4% -> 0% of each run, Pallas kernels for 0% -> 0%
where the time goes in v1:
time: 248 us
  Pallas kernels  192 us (77%)
  local copies, waits for them, and re-layouts  21.3 us (9%)
  matrix products  17 us (7%)
  other arithmetic  15.6 us (6%)
    pallas_call x1, Pallas kernels, gather_all(): pl.pallas_call(functools.partial(gather_kernel, chunks), out_shape=blocks...  80.3 us
    pallas_call x1, Pallas kernels, reduce_all(): pl.pallas_call(functools.partial(reduce_kernel, chunks, kinds), out_shape...  74.5 us
    pallas_call x1, Pallas kernels, attend_back(): pl.pallas_call(attend_back_kernel, grid=(2 * groups,), out_shape=[jax.Sha...  24.2 us
    pallas_call x1, Pallas kernels, attend(): pl.pallas_call(attend_kernel, grid=(2 * groups,), out_shape=[jax.ShapeDty...  13.4 us
    dot_general x6, matrix products, plain(): return jnp.dot(left_side, right_side, preferred_element_type=jnp.float32)  6.93 us
    dot_general x8, matrix products, contract_last(): lax.dot_general(left_side, right_side, (((1,), (1,)), ((), ())), preferre...  6.61 us

profile of v1, /device:TPU:0, one launch (start us, length us, event | category | flops | bytes accessed | tf_op | source)
XLA Modules:
  0.0 247.5 jit_solution(15441327608965883566)
XLA Ops:
  0.6 0.7 scatter.6
  1.4 0.7 scatter.9.refs_4_
  2.7 80.3 %shard_map.152 = (bf16[2,3,2,2,2,2,48,384]{7,6,5,4,3,2,1,0:T(8,128)(2,1)}, bf16[2,1,2,2,2,2,48,384]{7,6,5,4,3,2,1,0:T(8,128)(2,1)}, bf16[2,2,2,2,2,2,48,576]{7,6...) custom-call(bf16[3,48,384]{2,1,0:T(8,128)(2,1)} %refs_0_.1, ...), custom_call_target="tpu_custom_call" | custom-call | tf_op jit(solution)/shard_map/pallas_call | solution.py:157
  83.1 2.2 fusion.52
  85.4 0.9 slice.176
  87.6 1.2 multiply_convert_fusion.normed
  89.2 0.8 copy.23
  90.3 1.7 maximum_select_fusion.cosine
  92.0 0.8 copy.26
  93.1 1.7 maximum_select_fusion.1.sine
  94.8 0.8 copy.27.seg_rows
  95.6 13.4 %shard_map.153 = (bf16[256,768]{1,0:T(8,128)(2,1)}, bf16[512,768]{1,0:T(8,128)(2,1)}, bf16[512,768]{1,0:T(8,128)(2,1)}, bf16[256,768]{1,0:T(8,128)(2,1)}, f32[256,768]{1,0:T(8,128)}) custom-call(bf16[512,768]{1,0:T(8,128)(2,1)} %multiply_convert_fusion.normed, bf16[2,3,768,384]{3,2,1,0:T(8,128)(2,1)} %bitcast.101, bf16[2,3,768,384]{3,2,1,0:T(8,128)(2,1)} %bitcast.102, ...), custom_call_target="tpu_custom_call" | custom-call | tf_op jit(solution)/shard_map/pallas_call | solution.py:422
  109.0 1.4 convolution_add_fusion.1
  111.7 1.9 fusion.8
  114.5 0.8 copy-done.5
  115.4 1.8 multiply_convert_fusion.3
  118.8 1.8 multiply_convert_fusion.2
  120.7 1.3 fusion.6
  123.7 1.3 multiply_reduce_fusion.4
  125.0 1.3 fusion.48
  126.3 24.2 %shard_map.154 = (bf16[2,3,768,384]{3,2,1,0:T(8,128)(2,1)}, bf16[2,1,768,384]{3,2,1,0:T(8,128)(2,1)}, f32[512,768]{1,0:T(8,128)}) custom-call(bf16[512,768]{1,0:T(8,128)(2,1)} %multiply_convert_fusion.normed, bf16[256,768]{1,0:T(8,128)(2,1)} %get-tuple-element.78.branch, bf16[2,3,768,384]{3,2,1,0:T(8,128)(2,1)} %bitcast.104, ...), custom_call_target="tpu_custom_call" | custom-call | tf_op jit(solution)/shard_map/pallas_call | solution.py:446
  150.5 2.2 multiply_reduce_fusion
  152.8 1.7 subtract_multiply_fusion
  156.5 3.9 %copy.29 = bf16[4,768,576]{2,1,0:T(8,128)(2,1)} copy(bf16[4,768,576]{1,2,0:T(8,128)(2,1)S(1)} %pad_maximum_fusion) | data formatting | bytes 7077888 | tf_op jit(solution)/shard_map/stack | solution.py:557
  160.4 1.5 fusion.1
  163.7 1.6 pad_maximum_fusion.1.refs_3_
  166.2 0.8 slice.210.refs_5_
  167.0 74.5 %shard_map.155 = (f32[3,48,384]{2,1,0:T(8,128)}, f32[1,48,384]{2,1,0:T(8,128)}, f32[2,48,576]{2,1,0:T(8,128)}, f32[1,48,576]{2,1,0:T(8,128)}, f32[1,8,128]{2,1,0:T(8,128)}, /*index=5*/bf16[256,768]{1,0:T(8,128)(2,1)}) custom-call(bf16[2,3,2,2,2,2,48,384]{7,6,5,4,3,2,1,0:T(8,128)(2,1)} %bitcast.123, bf16[2,1,2,2,2,2,48,384]{7,6,5,4,3,2,1,0:T(8,128)(2,1)} %bitcast.126, ...), custom_call_target="tpu_custom_call" | custom-call | tf_op jit(solution)/shard_map/pallas_call | solution.py:296
  241.5 2.1 fusion.12
  243.6 1.3 slice_bitcast_fusion.12
  244.9 0.7 copy.42
  246.2 0.7 copy.44
  (104 shorter events, 14.3 us)
Async XLA Ops:
  0.6 84.7 %copy-start = (bf16[256,768]{1,0:T(8,128)(2,1)S(1)}, bf16[256,768]{1,0:T(8,128)(2,1)}, u32[]{:S(2)}) copy-start(bf16[256,768]{1,0:T(8,128)(2,1)} %refs_5_.1) | copy-start | bytes 1179652
  2.1 0.6 copy-start.20
  83.0 2.3 copy-start.2
  90.3 4.5 %copy-start.22 = (s32[512]{0:T(512)S(1)}, s32[512]{0:T(512)}, u32[]{:S(2)}) copy-start(s32[512]{0:T(512)} %param.14) | copy-start | bytes 6148
  94.8 0.8 copy-start.19
  109.0 1.4 copy-start.11
  109.0 1.4 copy-start.13
  110.4 0.7 copy-start.18
  111.2 2.4 copy-start.1
  111.6 2.7 %copy-start.12 = (bf16[2,1,2,2,2,2,48,576]{7,6,5,4,3,2,1,0:T(8,128)(2,1)S(1)}, bf16[2,1,2,2,2,2,48,576]{7,6,5,4,3,2,1,0:T(8,128)(2,1)}, u32[]{:S(2)}) copy-start(bf16[2,1,2,2,2,2,48,576]{7,6,5,4,3,2,1,0:T(8,128)(2,1)} %get-tuple-element.58) | copy-start | bytes 5308420
  114.4 1.0 copy-start.5
  117.2 1.1 copy-start.9
  120.7 2.4 copy-start.8
  150.5 2.3 copy-start.3
  160.4 2.2 copy-start.6
  160.4 2.2 copy-start.10
  163.7 1.6 copy-start.21
  163.7 2.5 %copy-start.4 = (f32[512,768]{1,0:T(8,128)S(1)}, f32[512,768]{1,0:T(8,128)}, u32[]{:S(2)}) copy-start(f32[512,768]{1,0:T(8,128)} %subtract_multiply_fusion) | copy-start | bytes 4718596
  167.0 74.5 %copy-start.7 = (f32[256,768]{1,0:T(8,128)S(1)}, f32[256,768]{1,0:T(8,128)}, u32[]{:S(2)}) copy-start(f32[256,768]{1,0:T(8,128)} %get-tuple-element.79) | copy-start | bytes 2359300
  241.5 3.4 %copy-start.15 = (f32[3,48,384]{2,1,0:T(8,128)S(1)}, f32[3,48,384]{2,1,0:T(8,128)}, u32[]{:S(2)}) copy-start(f32[3,48,384]{2,1,0:T(8,128)} %get-tuple-element.119) | copy-start | bytes 663556
  241.5 4.1 %copy-start.17 = (f32[1,48,384]{2,1,0:T(8,128)S(1)}, f32[1,48,384]{2,1,0:T(8,128)}, u32[]{:S(2)}) copy-start(f32[1,48,384]{2,1,0:T(8,128)} %get-tuple-element.69) | copy-start | bytes 221188
  241.5 4.7 %copy-start.14 = (f32[2,48,576]{2,1,0:T(8,128)S(1)}, f32[2,48,576]{2,1,0:T(8,128)}, u32[]{:S(2)}) copy-start(f32[2,48,576]{2,1,0:T(8,128)} %get-tuple-element.121) | copy-start | bytes 663556
  241.5 5.4 %copy-start.16 = (f32[1,48,576]{2,1,0:T(8,128)S(1)}, f32[1,48,576]{2,1,0:T(8,128)}, u32[]{:S(2)}) copy-start(f32[1,48,576]{2,1,0:T(8,128)} %get-tuple-element.71) | copy-start | bytes 331780
